TPU v7x, 512 devices: a whole 4x4x16 slice. The times are simulated.
512 devices in a mesh: replica: 32 (over x, z_lo, core), tensor: 16 (over z_hi, y).
Axes of the slice: x: 4, y: 4, z: 16 (z_hi: 4, z_lo: 4; z = z_hi * 4 + z_lo), core: 2. Of those that a mesh axis runs over, the one named last changes fastest.
Arguments:
- hidden_in: bfloat16 [4, 256, 2560], P(None, 'replica', 'tensor'), may hold values from -1500 to 1500
- norm_gain: float32 [2560], replicated, may hold values from 0.1 to 1.9
- w_query: bfloat16 [2560, 4096], P(None, 'tensor'), may hold values from -0.125 to 0.125
- w_keyval: bfloat16 [1024, 2560], P('tensor'), may hold values from -0.5 to 0.5
- w_out: bfloat16 [4096, 2560], P('tensor'), may hold values from -0.1875 to 0.1875
- query_input_factor: bfloat16 [64, 2560], P('replica'), may hold values from -0.125 to 0.125
- b_query: bfloat16 [64, 4096], P('replica', 'tensor'), may hold values from -0.25976562 to 0.25976562
- a_out: bfloat16 [64, 4096], P('replica', 'tensor'), may hold values from -0.1875 to 0.1875
- b_out: bfloat16 [64, 2560], P('replica'), may hold values from -0.25976562 to 0.25976562
- component_owner_rows: int32 [2, 64], replicated, may hold values from 0 to 63, each once within a row
- lengths: int32 [256], P('replica'), may hold values from 256 to 2048, as said below
- kv_cache: bfloat16 [256, 2048, 1024], P('replica', 'tensor'), may hold values from -1700 to 1700
Outputs:
- attention_out: bfloat16 [4, 256, 2560], P(None, 'replica', 'tensor')
Inputs may be any that keep to these rules, and one draw needn't show every extreme that they name: Positions lengths[b] and beyond of sequence b are unused; some sequence fills all 2048 positions.
All inputs are finite; a program needn't handle non-finite values.
Results may differ from a plain program's by a relative error of at most 0.02.
The roundings to bfloat16 on the way count: a program that leaves them out, or rounds other values in their place, can miss the bound.
Values may be sent and summed in bfloat16 or wider, within the bound.
A program may use at most 64 MiB of HBM per device.

v0:
```python
import jax
import jax.numpy as jnp
from jax import lax
from jax.sharding import PartitionSpec as P

HQ = 32
KVH = 4
HD = 128


adapter_scale = 2.0
norm_eps = 1e-06
masked_score = -1e30
highest = lax.Precision.HIGHEST


def pairing_order(component_owner_rows, adapter_rank_size):
    label_names = lax.broadcasted_iota(jnp.int32, (adapter_rank_size, adapter_rank_size), 1)
    first_rows = (component_owner_rows[0][:, None] == label_names).astype(jnp.float32)
    second_rows = (component_owner_rows[1][:, None] == label_names).astype(jnp.float32)
    return jnp.dot(first_rows.T, second_rows, precision=highest)


def body(
    hidden_in,
    norm_gain,
    w_query,
    w_keyval,
    w_out,
    query_input_factor,
    b_query,
    a_out,
    b_out,
    component_owner_rows,
    lengths,
    kv_cache,
):
    query_input_factor, b_query, a_out, b_out = (
        lax.all_gather(query_input_factor, "replica", axis=0, tiled=True),
        lax.all_gather(b_query, "replica", axis=0, tiled=True),
        lax.all_gather(a_out, "replica", axis=0, tiled=True),
        lax.all_gather(b_out, "replica", axis=0, tiled=True),
    )
    adapter_rank_size = query_input_factor.shape[0]
    paired_rows = pairing_order(component_owner_rows, adapter_rank_size) * adapter_scale
    lifted_query = jnp.dot(paired_rows, b_query.astype(jnp.float32), precision=highest)
    lifted_out = jnp.dot(paired_rows, b_out.astype(jnp.float32), precision=highest)
    device = lax.axis_index("tensor")
    heads_local = w_query.shape[1] // HD
    group_size = HQ // KVH
    local_positions = kv_cache.shape[1]
    score_scale = HD ** (-0.5)
    merged_query = w_query.astype(jnp.float32) + jnp.dot(
        query_input_factor.astype(jnp.float32).T, lifted_query, precision=highest
    )
    merged_out = w_out.astype(jnp.float32) + jnp.dot(
        a_out.astype(jnp.float32).T, lifted_out, precision=highest
    )
    cached = kv_cache.reshape(kv_cache.shape[0], local_positions, 2, KVH, HD)
    gathered = lax.all_gather(hidden_in, "tensor", axis=2, tiled=True)
    steps_here, sequences, model_width = gathered.shape
    flattened = gathered.reshape(steps_here * sequences, model_width).astype(jnp.float32)
    spread = lax.rsqrt(jnp.mean(flattened * flattened, axis=1, keepdims=True) + norm_eps)
    normed = (flattened * spread * norm_gain).astype(jnp.bfloat16)
    queries_local = jnp.dot(normed.astype(jnp.float32), merged_query, precision=highest).astype(
        jnp.bfloat16
    )
    fresh_local = jnp.einsum(
        "rd,cd->rc", normed, w_keyval, preferred_element_type=jnp.float32
    ).astype(jnp.bfloat16)
    queries, keyvals = (
        lax.all_gather(
            queries_local.reshape(steps_here, sequences, -1), "tensor", axis=2, tiled=True
        ),
        lax.all_gather(
            fresh_local.reshape(steps_here, sequences, -1), "tensor", axis=2, tiled=True
        ),
    )
    head_rows = queries.reshape(steps_here, sequences, KVH, group_size, HD)
    scores = (
        jnp.einsum(
            "nskgd,spkd->nskgp", head_rows, cached[:, :, 0], preferred_element_type=jnp.float32
        )
        * score_scale
    )
    position = device * local_positions + lax.broadcasted_iota(
        jnp.int32, (sequences, local_positions), 1
    )
    usable = (position < lengths[:, None])[None, :, None, None, :]
    scores = jnp.where(usable, scores, masked_score)
    block_max = jnp.max(scores, axis=4)
    appended = keyvals.reshape(steps_here, sequences, 2, KVH, HD)
    recent = (
        jnp.einsum(
            "nskgd,mskd->nskgm", head_rows, appended[:, :, 0], preferred_element_type=jnp.float32
        )
        * score_scale
    )
    current = lax.broadcasted_iota(jnp.int32, (steps_here, steps_here), 0)
    previous = lax.broadcasted_iota(jnp.int32, (steps_here, steps_here), 1)
    causal = (current >= previous)[:, None, None, None, :]
    recent = jnp.where(causal, recent, masked_score)
    weights = jnp.where(usable, jnp.exp(scores - block_max[..., None]), 0.0)
    totals = jnp.sum(weights, axis=4)
    partial_value = jnp.einsum(
        "nskgp,spkd->nskgd",
        weights.astype(jnp.bfloat16),
        cached[:, :, 1],
        preferred_element_type=jnp.float32,
    )
    first_head = device * heads_local
    own_group = first_head // group_size
    recent_own = lax.dynamic_slice_in_dim(
        recent.reshape(steps_here, sequences, HQ, steps_here), first_head, heads_local, 2
    )
    peak = lax.pmax(block_max, "tensor")
    maxima = jnp.maximum(peak, jnp.max(recent, axis=4))
    block_scale = jnp.exp(block_max - maxima)
    partial_value = partial_value * block_scale[..., None]
    totals = totals * block_scale
    partial_value, totals = (
        lax.psum_scatter(
            partial_value.reshape(steps_here, sequences, HQ, HD).astype(jnp.bfloat16),
            "tensor",
            scatter_dimension=2,
            tiled=True,
        ).astype(jnp.float32),
        lax.psum_scatter(
            totals.reshape(steps_here, sequences, HQ).astype(jnp.bfloat16),
            "tensor",
            scatter_dimension=2,
            tiled=True,
        ).astype(jnp.float32),
    )
    maxima_own = lax.dynamic_slice_in_dim(
        maxima.reshape(steps_here, sequences, HQ), first_head, heads_local, 2
    )
    fresh_weights = jnp.exp(recent_own - maxima_own[..., None])
    fresh_values = lax.dynamic_index_in_dim(appended[:, :, 1], own_group, 2, keepdims=False)
    totals = totals + jnp.sum(fresh_weights, axis=3)
    partial_value = partial_value + jnp.einsum(
        "nshm,msd->nshd",
        fresh_weights.astype(jnp.bfloat16),
        fresh_values,
        preferred_element_type=jnp.float32,
    )
    mixed_heads = (
        (partial_value / totals[..., None])
        .astype(jnp.bfloat16)
        .reshape(steps_here * sequences, heads_local * HD)
    )
    summed = lax.psum_scatter(
        jnp.einsum(
            "rh,hc->cr", mixed_heads.astype(jnp.float32), merged_out, precision=highest
        ).astype(jnp.bfloat16),
        "tensor",
        scatter_dimension=0,
        tiled=True,
    ).astype(jnp.float32)
    return summed.T.reshape(steps_here, sequences, -1).astype(jnp.bfloat16)


def solution(mesh):
    return jax.shard_map(
        body,
        mesh=mesh,
        in_specs=(
            P(None, "replica", "tensor"),
            P(),
            P(None, "tensor"),
            P("tensor", None),
            P("tensor", None),
            P("replica", None),
            P("replica", "tensor"),
            P("replica", "tensor"),
            P("replica", None),
            P(),
            P("replica"),
            P("replica", "tensor", None),
        ),
        out_specs=P(None, "replica", "tensor"),
        check_vma=False,
    )
```

profile of v0, /device:TPU:2, one launch (start us, length us, event | category | flops | bytes accessed | tf_op | source)
XLA Modules:
  0.0 757.3 jit_solution(18190599333178603839)
XLA Ops:
  6.6 0.5 iota_compare_fusion.4
  7.1 0.8 slice_bitcast_fusion.5
  7.8 37.7 %all-gather.2 = bf16[32,2,256]{2,1,0:T(2,128)(2,1)S(1)} all-gather(bf16[1,2,256]{2,1,0:T(2,128)(2,1)} %bitcast.128), channel_id=1, replica_groups=mesh['replica'=32,'tensor'=16] {'replica'}, dimensions={0}, use_global_device_ids=true | all-gather | bytes 33792 | tf_op jit(solution)/shard_map/all_gather | solution.py:40
  45.5 2.4 copy.100
  48.0 39.6 %all-gather.3 = bf16[32,2,2560]{2,1,0:T(2,128)(2,1)S(1)} all-gather(bf16[1,2,2560]{2,1,0:T(2,128)(2,1)S(1)} %bitcast.126), channel_id=1, replica_groups=mesh['replica'=32,'tensor'=16] {'replica'}, dimensions={0}, use_global_device_ids=true | all-gather | bytes 337920 | tf_op jit(solution)/shard_map/all_gather | solution.py:39
  87.5 0.1 reshape.106
  87.7 0.1 copy.98
  87.8 138.9 %all_gather.23 = bf16[4,8,2560]{1,0,2:T(4,128)(2,1)S(1)} all-gather(bf16[4,8,160]{1,0,2:T(4,128)(2,1)S(1)} %copy.98), channel_id=1, replica_groups=mesh['replica'=32,'tensor'=16] {'tensor'}, dimensions={2}, use_global_device_ids=true | all-gather | bytes 174080 | tf_op jit(solution)/shard_map/all_gather | solution.py:60
  226.7 1.4 copy.99
  228.1 0.1 fusion.15
  228.3 0.3 convolution_multiply_fusion.2
  228.6 0.6 copy-done.8
  229.2 0.2 fusion.41
  229.4 2.6 fusion
  232.0 1.4 fusion.8
  233.5 46.7 %all_gather.26 = bf16[4,8,4096]{2,1,0:T(8,128)(2,1)S(1)} all-gather(bf16[4,8,256]{2,1,0:T(8,128)(2,1)S(1)} %fusion.8), channel_id=1, replica_groups=mesh['replica'=32,'tensor'=16] {'tensor'}, dimensions={2}, use_global_device_ids=true | all-gather | bytes 278528 | tf_op jit(solution)/shard_map/all_gather | solution.py:72
  280.2 2.4 copy.101
  282.7 1.7 fusion.38
  284.4 94.1 %pmax.7 = f32[4,8,4,8]{3,0,2,1:T(4,128)} all-reduce(f32[4,8,4,8]{3,0,2,1:T(4,128)S(1)} %get-tuple-element.14), channel_id=1, replica_groups=mesh['replica'=32,'tensor'=16] {'tensor'}, use_global_device_ids=true, to_apply=%region_2.3 | all-reduce | flops 1024 | bytes 8192 | tf_op jit(solution)/shard_map/pmax | solution.py:116
  378.5 1.1 fusion.10
  379.6 0.3 fusion.9
  379.8 0.7 copy.105
  380.6 63.2 %all_gather.27 = bf16[4,8,1024]{1,0,2:T(4,128)(2,1)S(1)} all-gather(bf16[4,8,64]{1,0,2:T(4,128)(2,1)} %copy.105), channel_id=1, replica_groups=mesh['replica'=32,'tensor'=16] {'tensor'}, dimensions={2}, use_global_device_ids=true | all-gather | bytes 69632 | tf_op jit(solution)/shard_map/all_gather | solution.py:75
  443.8 1.2 copy.106
  445.0 1.4 fusion.37
  446.4 3.0 fusion.39
  449.4 1.5 multiply_convert_fusion
  450.9 1.8 fusion.5
  452.8 0.8 copy.110
  453.7 0.9 copy.114
  454.6 1.1 copy.113
  455.7 0.2 reshape.95
  456.1 0.9 copy.125
  457.0 93.4 %all-reduce = bf16[4,8,32]{1,0,2:T(4,128)(2,1)S(1)} all-reduce(bf16[4,8,32]{1,0,2:T(4,128)(2,1)S(1)} %bitcast.125), channel_id=3, replica_groups=mesh['replica'=32,'tensor'=16] {'tensor'}, use_global_device_ids=true, to_apply=%region_6.7.clone | all-reduce | flops 1024 | bytes 4096
  550.4 1.3 dynamic-slice.1
  552.3 0.3 copy.115
  552.6 38.4 %all-gather = bf16[32,2,2560]{2,1,0:T(2,128)(2,1)S(1)} all-gather(bf16[1,2,2560]{2,1,0:T(2,128)(2,1)S(1)} %bitcast.127), channel_id=1, replica_groups=mesh['replica'=32,'tensor'=16] {'replica'}, dimensions={0}, use_global_device_ids=true | all-gather | bytes 337920 | tf_op jit(solution)/shard_map/all_gather | solution.py:42
  591.0 0.1 reshape.100
  591.2 1.3 fusion.40
  592.4 1.4 copy.97
  593.9 34.0 %all-gather.1 = bf16[32,2,256]{2,1,0:T(2,128)(2,1)S(1)} all-gather(bf16[1,2,256]{2,1,0:T(2,128)(2,1)S(1)} %bitcast.129), channel_id=1, replica_groups=mesh['replica'=32,'tensor'=16] {'replica'}, dimensions={0}, use_global_device_ids=true | all-gather | bytes 33792 | tf_op jit(solution)/shard_map/all_gather | solution.py:41
  627.9 0.7 constant_dynamic-slice_fusion.1
  628.6 0.1 fusion.33
  628.8 2.7 fusion.1
  631.5 2.2 convolution_convert_fusion
  633.7 1.1 copy.126
  634.8 114.2 %reduce-scatter.7.cloned.1.call-done = bf16[160,32]{1,0:T(8,128)(2,1)} async-done(((bf16[2560,32]{1,0:T(8,128)(2,1)}), bf16[160,32]{1,0:T(8,128)(2,1)}) %reduce-scatter.7.cloned.1.call-update) | async-done | bytes 10256
  749.0 1.5 copy.127
  (53 shorter events, 0.8 us)
Async XLA Ops:
  6.5 373.0 %copy-start = (bf16[64,2560]{1,0:T(8,128)(2,1)S(1)}, bf16[64,2560]{1,0:T(8,128)(2,1)}, u32[]{:S(2)}) copy-start(bf16[64,2560]{1,0:T(8,128)(2,1)} %param.15) | copy-start | bytes 983044
  6.5 41.4 %copy-start.12 = (bf16[2,2560]{1,0:T(2,128)(2,1)S(1)}, bf16[2,2560]{1,0:T(2,128)(2,1)}, u32[]{:S(2)}) copy-start(bf16[2,2560]{1,0:T(2,128)(2,1)} %param.17) | copy-start | bytes 30724
  6.5 81.1 %copy-start.10 = (bf16[4,8,160]{2,1,0:T(8,128)(2,1)S(1)}, bf16[4,8,160]{2,1,0:T(8,128)(2,1)}, u32[]{:S(2)}) copy-start(bf16[4,8,160]{2,1,0:T(8,128)(2,1)} %param.12) | copy-start | bytes 30724
  6.5 625.0 %reduce-scatter.5.cloned.1.call-start = ((), (), s32[]{:S(2)}) async-start(), calls=%async_computation.2 | async-start | bytes 278528 | tf_op jit(solution)/shard_map/reduce_scatter | solution.py:122
  228.1 5.4 copy-start.3
  228.1 3.9 copy-start.11
  228.3 5.1 copy-start.14
  228.6 0.6 copy-start.8
  232.0 48.2 %copy-start.1 = (bf16[8,128,1024]{2,1,0:T(8,128)(2,1)S(1)}, bf16[8,128,1024]{2,1,0:T(8,128)(2,1)}, u32[]{:S(2)}) copy-start(bf16[8,128,1024]{2,1,0:T(8,128)(2,1)} %param.23) | copy-start | bytes 6291460
  233.5 49.1 %copy-start.17 = (s32[8]{0:T(128)S(1)}, s32[8]{0:T(128)}, u32[]{:S(2)}) copy-start(s32[8]{0:T(128)} %param.22) | copy-start | bytes 100
  280.2 2.5 copy-start.7
  282.6 97.0 %copy-start.4 = (bf16[4,8,2560]{2,1,0:T(8,128)(2,1)S(1)}, bf16[4,8,2560]{2,1,0:T(8,128)(2,1)}, u32[]{:S(2)}) copy-start(bf16[4,8,2560]{2,1,0:T(8,128)(2,1)} %copy-done.3) | copy-start | bytes 491524
  282.6 97.0 %copy-start.15 = (f32[32]{0:T(128)S(1)}, f32[32]{0:T(128)}, u32[]{:S(2)}) copy-start(f32[32]{0:T(128)} %copy-done.14) | copy-start | bytes 388
  284.4 95.4 %copy-start.6 = (f32[4,8,4,8,128]{4,3,0,2,1:T(8,128)}, f32[4,8,4,8,128]{4,3,0,2,1:T(8,128)S(1)}, u32[]{:S(2)}) copy-start(f32[4,8,4,8,128]{4,3,0,2,1:T(8,128)S(1)} %get-tuple-element.15) | copy-start | bytes 1572868
  284.4 166.5 %copy-start.2 = (bf16[8,128,1024]{1,2,0:T(8,128)(2,1)S(1)}, bf16[8,128,1024]{1,2,0:T(8,128)(2,1)}, u32[]{:S(2)}) copy-start(bf16[8,128,1024]{1,2,0:T(8,128)(2,1)} %copy.101) | copy-start | bytes 6291460
  450.9 101.7 %copy-start.13 = (bf16[2,2560]{1,0:T(2,128)(2,1)S(1)}, bf16[2,2560]{1,0:T(2,128)(2,1)}, u32[]{:S(2)}) copy-start(bf16[2,2560]{1,0:T(2,128)(2,1)} %param.20) | copy-start | bytes 30724
  452.7 138.5 %copy-start.9 = (f32[64,64]{1,0:T(8,128)S(1)}, f32[64,64]{1,0:T(8,128)}, u32[]{:S(2)}) copy-start(f32[64,64]{1,0:T(8,128)} %copy-done.8) | copy-start | bytes 49156
  452.7 139.7 %copy-start.5 = (bf16[256,2560]{1,0:T(8,128)(2,1)S(1)}, bf16[256,2560]{1,0:T(8,128)(2,1)}, u32[]{:S(2)}) copy-start(bf16[256,2560]{1,0:T(8,128)(2,1)} %param.16) | copy-start | bytes 3932164
  453.6 295.4 %reduce-scatter.7.cloned.1.call-start = ((), (), s32[]{:S(2)}) async-start(), calls=%async_computation.3 | async-start | bytes 696320
  455.8 138.0 %copy-start.16 = (bf16[2,256]{1,0:T(2,128)(2,1)S(1)}, bf16[2,256]{1,0:T(2,128)(2,1)}, u32[]{:S(2)}) copy-start(bf16[2,256]{1,0:T(2,128)(2,1)} %param.19) | copy-start | bytes 3076
Sparse Core Ops, SparseCore 0:
  453.7 108.2 reduce-scatter.4
  634.9 114.0 reduce-scatter.6
where the time goes:
time: 758 us; the launch traced here: 757 us
  blocking collectives  586 us (77%)
  waiting for transfers between devices  114 us (15%)
  local copies, waits for them, and re-layouts  21.8 us (3%)
  matrix products  17.5 us (2%)
  between operations  14.4 us (2%)
    all_gather x1, blocking collectives, body(): gathered = lax.all_gather(hidden_in, 'tensor', axis=2, tiled=True)  139 us
    unnamed x3, waiting for transfers between devices  114 us
    pmax x1, blocking collectives, body(): peak = lax.pmax(block_max, 'tensor')  94.1 us
    unnamed x1, blocking collectives  93.4 us
    all_gather x1, blocking collectives, body(): lax.all_gather(fresh_local.reshape(steps_here, sequences, -1), 'tensor',...  63.2 us
    all_gather x1, blocking collectives, body(): lax.all_gather(queries_local.reshape(steps_here, sequences, -1), 'tensor'...  46.7 us
    all_gather x1, blocking collectives, body(): lax.all_gather(query_input_factor, 'replica', axis=0, tiled=True)  39.6 us
    all_gather x1, blocking collectives, body(): lax.all_gather(b_out, 'replica', axis=0, tiled=True)  38.4 us
  transfers between devices with their start and end apart: 2, of which 1 were waited for; matrix products, arithmetic and copies ran while one was open for 1% of the time, Pallas kernels for 0%

commit v1 on v0

v1 whole, which is shorter than its diff:
```python
import jax
import jax.numpy as jnp
from jax import lax
from jax.experimental import pallas as pl
from jax.experimental.pallas import tpu as pltpu
from jax.sharding import PartitionSpec as P

HQ = 32
KVH = 4
HD = 128
STEPS = 4
SEQ = 8
D = 2560
NT = 16
NR = 32
RANK = 64
FEAT = D // NT
TOK = STEPS * SEQ
POS = 128
ROWS = TOK * 2
GROUP = HQ // KVH
CHUNKS = D // 128

adapter_scale = 2.0
norm_eps = 1e-06
masked_score = -1e30

F32 = jnp.float32
BF16 = jnp.bfloat16
MESH = pl.DeviceIdType.MESH


def dot(a, b):
    return jnp.dot(a, b, preferred_element_type=F32)


def dot_nt(a, b):
    return lax.dot_general(a, b, (((1,), (1,)), ((), ())), preferred_element_type=F32)


def split(x):
    hi = x.astype(BF16)
    return hi, (x - hi.astype(F32)).astype(BF16)


def iota(shape, dim):
    return lax.broadcasted_iota(jnp.int32, shape, dim)


def kernel(
    hid_hbm, gain_hbm, wq_hbm, wkv_hbm, wo_hbm, qif_hbm, bq_hbm, ao_hbm, bo_hbm, own_hbm, len_hbm, kv_hbm,
    out_ref,
    hid, gain, wq, wkv, wo, wide, narrow, own, lens, kv,
    hid_all, asm, pack, ad_send, ad_all, ad_f32, qi_mat, bq_mat, ao_mat, bo_mat,
    qf32, q_send, q_all, fresh_send, fresh_all,
    o_send, o_all, st_mat, st_send, st_all, mix, part, e_send, e_all,
    ld, own_sem, b_s, b_r, a_s, a_r, q_s, q_r, f_s, f_r, o_s, o_r, t_s, t_r, e_s, e_r,
):
    t = lax.axis_index("tensor")
    r = lax.axis_index("replica")

    def loads():
        pairs = [
            (hid_hbm, hid), (qif_hbm, wide.at[0]), (bq_hbm, narrow.at[0]), (ao_hbm, narrow.at[1]), (bo_hbm, wide.at[1]),
            (own_hbm, own), (len_hbm, lens), (gain_hbm, gain), (wq_hbm, wq), (wkv_hbm, wkv), (kv_hbm, kv), (wo_hbm, wo),
        ]
        return [pltpu.make_async_copy(a, b, ld.at[i]) for i, (a, b) in enumerate(pairs)]

    load = loads()
    for c in load:
        c.start()

    barrier = pltpu.get_barrier_semaphore()
    for d in range(1, NT):
        pl.semaphore_signal(barrier, inc=1, device_id={"tensor": lax.rem(t + d, NT)}, device_id_type=MESH)
    for d in range(1, NR):
        pl.semaphore_signal(barrier, inc=1, device_id={"replica": lax.rem(r + d, NR)}, device_id_type=MESH)

    for c in load[1:5]:
        c.wait()
    for j in range(2):
        pack[...] = jnp.zeros_like(pack)
        x = wide[j].astype(F32)
        for c in range(CHUNKS):
            pack[2 * c : 2 * c + 2, :] = x[:, 128 * c : 128 * c + 128]
        y = narrow[j].astype(F32)
        for c in range(2):
            pack[2 * (CHUNKS + c) : 2 * (CHUNKS + c) + 2, :] = y[:, 128 * c : 128 * c + 128]
        ad_send[j] = pack[...].astype(BF16)
    load[0].wait()
    pl.semaphore_wait(barrier, NT - 1 + NR - 1)

    sends = []

    def send_tensor(src, dst, ss, rs, d):
        peer = lax.rem(t + d, NT)
        c = pltpu.make_async_remote_copy(
            src_ref=src(peer), dst_ref=dst.at[t], send_sem=ss.at[d], recv_sem=rs.at[t],
            device_id={"tensor": peer}, device_id_type=MESH,
        )
        c.start()
        sends.append(c)

    far_first = [8, 7, 9, 6, 10, 5, 11, 4, 12, 3, 13, 2, 14, 1, 15]

    def send_all_tensor(src, dst, ss, rs):
        for d in far_first:
            send_tensor(src, dst, ss, rs, d)
        pltpu.make_async_copy(src(t), dst.at[t], rs.at[t]).start()

    def arrived(dst, rs, i):
        pltpu.make_async_copy(dst.at[i], dst.at[i], rs.at[i]).wait()

    def send_adapters(j):
        for d in range(1, NR):
            c = pltpu.make_async_remote_copy(
                src_ref=ad_send.at[j], dst_ref=ad_all.at[j, r], send_sem=a_s.at[j, d], recv_sem=a_r.at[j, r],
                device_id={"replica": lax.rem(r + d, NR)}, device_id_type=MESH,
            )
            c.start()
            sends.append(c)
        pltpu.make_async_copy(ad_send.at[j], ad_all.at[j, r], a_r.at[j, r]).start()

    def take_adapters(j, wide_mat, narrow_mat):
        for s in range(NR):
            arrived(ad_all.at[j], a_r.at[j], s)
        for s in range(NR):
            ad_f32[48 * s : 48 * s + 48, :] = ad_all[j, s].astype(F32)
        for c in range(CHUNKS + 2):
            rows = [ad_f32[pl.ds(2 * c + i, NR, stride=48), :] for i in range(2)]
            block = jnp.concatenate(rows, axis=0).astype(BF16)
            if c < CHUNKS:
                wide_mat[:, 128 * c : 128 * c + 128] = block
            else:
                narrow_mat[:, 128 * (c - CHUNKS) : 128 * (c - CHUNKS) + 128] = block

    send_all_tensor(lambda p: hid, hid_all, b_s, b_r)
    send_adapters(0)

    for c in load[5:]:
        c.wait()

    label = iota((RANK, RANK), 0)
    label = lax.rem(label, NR) * 2 + label // NR
    first = (label == own[0:1, :]).astype(F32).astype(BF16)
    second = (label == own[1:2, :]).astype(F32).astype(BF16)
    paired = (dot_nt(first, second) * adapter_scale).astype(BF16)

    squares = jnp.zeros((TOK, 1), F32)
    for s in range(NT):
        arrived(hid_all, b_r, s)
        x = hid_all[s].astype(F32)
        asm[:, FEAT * s : FEAT * (s + 1)] = x
        squares = squares + jnp.sum(x * x, axis=1, keepdims=True)
    spread = lax.rsqrt(squares * (1.0 / D) + norm_eps)
    normed = (asm[...] * spread * gain[...]).astype(BF16)

    queries = dot(normed, wq[...])
    fresh = dot_nt(normed, wkv[...]).astype(BF16).astype(F32)
    take_adapters(0, qi_mat, bq_mat)
    low_hi, low_lo = split(dot_nt(normed, qi_mat[...]))
    lifted = dot(paired, bq_mat[...]).astype(BF16)
    queries = queries + (dot(low_hi, lifted) + dot(low_lo, lifted))

    for n in range(STEPS):
        for h in range(2):
            qf32[pl.ds(n * 2 + h, SEQ, stride=8), :] = queries[n * SEQ : (n + 1) * SEQ, h * HD : (h + 1) * HD]
    q_send[...] = qf32[...].astype(BF16)
    send_all_tensor(lambda p: q_send, q_all, q_s, q_r)

    zeros = jnp.zeros((TOK, 64), F32)
    left = jnp.concatenate([fresh, zeros], axis=1)
    right = jnp.concatenate([zeros, fresh], axis=1)
    half = lax.rem(t, 2)
    fresh_send[...] = jnp.where(half == 0, left, right).astype(BF16)
    slot = (t // 8) * 2 + half
    head_row = lax.rem(t, 8) // 2
    for y in range(4):
        peer = head_row * 4 + y
        remote = pltpu.make_async_remote_copy(
            src_ref=fresh_send, dst_ref=fresh_all.at[slot], send_sem=f_s.at[y], recv_sem=f_r.at[slot],
            device_id={"tensor": peer}, device_id_type=MESH,
        )
        local = pltpu.make_async_copy(fresh_send, fresh_all.at[slot], f_r.at[slot])

        @pl.when(peer != t)
        def _():
            remote.start()

        @pl.when(peer == t)
        def _():
            local.start()

    send_adapters(1)

    lane = iota((4 * 16, 2 * POS), 1)
    row = iota((4 * 16, 2 * POS), 0)
    same = (lane // POS) == (lax.rem(row, 16) // 8)
    position = lax.rem(lane, POS) + t * POS
    stat_lane = iota((16, 128), 1)
    usables = []
    for p in range(4):
        limit = jnp.where(lane < POS, lens[2 * p], lens[2 * p + 1])
        usables.append(same & (position < limit))
    maxes = [jnp.full((16, 128), masked_score, F32) for _ in range(4)]
    sums = [jnp.zeros((16, 128), F32) for _ in range(4)]
    score_scale = HD ** (-0.5)
    for k in range(KVH):
        for y in range(4):
            arrived(q_all, q_r, 4 * k + y)
        for p in range(4):
            usable = usables[p]
            lhs = jnp.concatenate([q_all[4 * k + y, 16 * p : 16 * p + 16, :] for y in range(4)], axis=0)
            keys = kv[2 * p : 2 * p + 2, :, HD * k : HD * (k + 1)].reshape(2 * POS, HD)
            values = kv[2 * p : 2 * p + 2, :, HD * (KVH + k) : HD * (KVH + k + 1)].reshape(2 * POS, HD)
            scores = jnp.where(usable, dot_nt(lhs, keys) * score_scale, masked_score)
            top = jnp.max(scores, axis=1, keepdims=True)
            weights = jnp.where(usable, jnp.exp(scores - top), 0.0)
            total = jnp.sum(weights, axis=1, keepdims=True)
            mixed = dot(weights.astype(BF16), values).astype(BF16)
            for y in range(4):
                i = 4 * k + y
                o_send[i, 16 * p : 16 * p + 16, :] = mixed[16 * y : 16 * y + 16, :]
                maxes[p] = jnp.where(stat_lane == i, top[16 * y : 16 * y + 16, :], maxes[p])
                sums[p] = jnp.where(stat_lane == i, total[16 * y : 16 * y + 16, :], sums[p])
    for p in range(4):
        st_mat[16 * p : 16 * p + 16, :] = maxes[p]
        st_mat[64 + 16 * p : 64 + 16 * p + 16, :] = sums[p]
    stats = jnp.transpose(st_mat[...])
    for i in range(NT):
        st_send[i] = stats[i : i + 1, :]
    send_all_tensor(lambda p: st_send.at[p], st_all, t_s, t_r)
    send_all_tensor(lambda p: o_send.at[p], o_all, o_s, o_r)

    for j in range(4):
        arrived(fresh_all, f_r, j)
    new_keys = fresh_all[0] + fresh_all[1]
    new_values = fresh_all[2] + fresh_all[3]
    row = iota((ROWS, TOK), 0)
    col = iota((ROWS, TOK), 1)
    causal = (lax.rem(col, SEQ) == row // 8) & (col // SEQ <= lax.rem(row, 8) // 2)
    recent = jnp.where(causal, dot_nt(q_send[...], new_keys) * score_scale, masked_score)
    recent_top = jnp.max(recent, axis=1, keepdims=True)

    take_adapters(1, bo_mat, ao_mat)
    lifted_out = dot(paired, bo_mat[...]).astype(BF16)

    for i in range(NT):
        arrived(st_all, t_r, i)
    st_mat[...] = jnp.full_like(st_mat, masked_score)
    for i in range(NT):
        st_mat[i : i + 1, :] = st_all[i]
    stats = jnp.transpose(st_mat[...])
    tops = stats[0:ROWS, :]
    valid = iota((ROWS, 128), 1) < NT
    totals = jnp.where(valid, stats[ROWS : 2 * ROWS, :], 0.0)
    peak = jnp.maximum(jnp.max(tops, axis=1, keepdims=True), recent_top)
    factor = jnp.where(valid, jnp.exp(tops - peak), 0.0)
    recent_weights = jnp.where(causal, jnp.exp(recent - peak), 0.0)
    total = jnp.sum(totals * factor, axis=1, keepdims=True) + jnp.sum(recent_weights, axis=1, keepdims=True)
    acc = dot(recent_weights.astype(BF16), new_values)
    for i in range(NT):
        arrived(o_all, o_r, i)
        acc = acc + o_all[i].astype(F32) * factor[:, i : i + 1]
    mix[...] = acc / total
    mixed = jnp.concatenate(
        [
            jnp.concatenate([mix[pl.ds(n * 2 + h, SEQ, stride=8), :] for h in range(2)], axis=1)
            for n in range(STEPS)
        ],
        axis=0,
    ).astype(BF16)

    low_hi, low_lo = split(dot_nt(mixed, ao_mat[...]))
    part[...] = dot(mixed, wo[...]) + (dot(low_hi, lifted_out) + dot(low_lo, lifted_out))
    for i in range(NT):
        e_send[i] = part[:, FEAT * i : FEAT * (i + 1)].astype(BF16)
    send_all_tensor(lambda p: e_send.at[p], e_all, e_s, e_r)
    summed = jnp.zeros((TOK, FEAT), F32)
    for i in range(NT):
        arrived(e_all, e_r, i)
        summed = summed + e_all[i].astype(F32)
    out_ref[...] = summed.astype(BF16)

    for c in sends:
        c.wait_send()
    for y in range(4):
        peer = head_row * 4 + y
        remote = pltpu.make_async_remote_copy(
            src_ref=fresh_send, dst_ref=fresh_all.at[slot], send_sem=f_s.at[y], recv_sem=f_r.at[slot],
            device_id={"tensor": peer}, device_id_type=MESH,
        )

        @pl.when(peer != t)
        def _():
            remote.wait_send()


def body(
    hidden_in, norm_gain, w_query, w_keyval, w_out, query_input_factor, b_query, a_out, b_out,
    component_owner_rows, lengths, kv_cache,
):
    dma = pltpu.SemaphoreType.DMA
    vmem = pltpu.VMEM
    scratch = [
        vmem((TOK, FEAT), BF16),
        vmem((1, D), F32),
        vmem((D, 256), BF16),
        vmem((64, D), BF16),
        vmem((256, D), BF16),
        vmem((2, 2, D), BF16),
        vmem((2, 2, 256), BF16),
        vmem((2, RANK), jnp.int32),
        pltpu.SMEM((SEQ,), jnp.int32),
        vmem((SEQ, POS, 1024), BF16),
        vmem((NT, TOK, FEAT), BF16),
        vmem((TOK, D), F32),
        vmem((48, 128), F32),
        vmem((2, 48, 128), BF16),
        vmem((2, NR, 48, 128), BF16),
        vmem((NR * 48, 128), F32),
        vmem((RANK, D), BF16),
        vmem((RANK, 256), BF16),
        vmem((RANK, 256), BF16),
        vmem((RANK, D), BF16),
        vmem((ROWS, HD), F32),
        vmem((ROWS, HD), BF16),
        vmem((NT, ROWS, HD), BF16),
        vmem((TOK, 128), BF16),
        vmem((4, TOK, 128), BF16),
        vmem((NT, ROWS, HD), BF16),
        vmem((NT, ROWS, HD), BF16),
        vmem((128, 128), F32),
        vmem((NT, 1, 128), F32),
        vmem((NT, 1, 128), F32),
        vmem((ROWS, HD), F32),
        vmem((TOK, D), F32),
        vmem((NT, TOK, FEAT), BF16),
        vmem((NT, TOK, FEAT), BF16),
        dma((12,)), dma((1,)),
        dma((NT,)), dma((NT,)),
        dma((2, NR)), dma((2, NR)),
        dma((NT,)), dma((NT,)),
        dma((4,)), dma((4,)),
        dma((NT,)), dma((NT,)),
        dma((NT,)), dma((NT,)),
        dma((NT,)), dma((NT,)),
    ]
    out = pl.pallas_call(
        kernel,
        out_shape=jax.ShapeDtypeStruct((TOK, FEAT), BF16),
        in_specs=[pl.BlockSpec(memory_space=pltpu.HBM)] * 12,
        out_specs=pl.BlockSpec(memory_space=pltpu.VMEM),
        scratch_shapes=scratch,
        compiler_params=pltpu.CompilerParams(collective_id=0, has_side_effects=True, vmem_limit_bytes=48 << 20),
    )(
        hidden_in.reshape(TOK, FEAT), norm_gain.reshape(1, D), w_query, w_keyval, w_out, query_input_factor, b_query,
        a_out, b_out, component_owner_rows, lengths, kv_cache,
    )
    return out.reshape(STEPS, SEQ, FEAT)


def solution(mesh):
    return jax.shard_map(
        body,
        mesh=mesh,
        in_specs=(
            P(None, "replica", "tensor"),
            P(),
            P(None, "tensor"),
            P("tensor", None),
            P("tensor", None),
            P("replica", None),
            P("replica", "tensor"),
            P("replica", "tensor"),
            P("replica", None),
            P(),
            P("replica"),
            P("replica", "tensor", None),
        ),
        out_specs=P(None, "replica", "tensor"),
        check_vma=False,
    )
```

time: 758 us -> 107 us (0.14)
  the two profiles are of different devices: /device:TPU:2 before, /device:TPU:32 now
where the time goes in v1:
time: 107 us; the launch traced here: 106 us
  Pallas kernels  95 us (89%)
  local copies, waits for them, and re-layouts  11.3 us (11%)
    pallas_call x1, Pallas kernels, body(): pl.pallas_call(kernel, out_shape=jax.ShapeDtypeStruct((TOK, FEAT), BF16),...  95 us
    unnamed x23, local copies, waits for them, and re-layouts  10.6 us

profile of v1, /device:TPU:32, one launch (start us, length us, event | category | flops | bytes accessed | tf_op | source)
XLA Modules:
  0.0 106.4 jit_solution(5636657038159164639)
XLA Ops:
  0.0 0.7 reshape.10.gain_hbm
  0.7 0.0 copy-start
  0.7 1.6 %copy-done = bf16[8,128,1024]{2,1,0:T(8,128)(2,1)S(1)} copy-done((bf16[8,128,1024]{2,1,0:T(8,128)(2,1)S(1)}, bf16[8,128,1024]{2,1,0:T(8,128)(2,1)}, u32[]{:S(2)}) %copy-start) | copy-done | bytes 2097176
  2.3 0.0 copy-start.1
  2.3 1.3 %copy-done.1 = bf16[2560,256]{1,0:T(8,128)(2,1)S(1)} copy-done((bf16[2560,256]{1,0:T(8,128)(2,1)S(1)}, bf16[2560,256]{1,0:T(8,128)(2,1)}, u32[]{:S(2)}) %copy-start.1) | copy-done | bytes 1310744
  3.6 0.0 copy-start.2
  3.6 1.3 %copy-done.2 = bf16[256,2560]{1,0:T(8,128)(2,1)S(1)} copy-done((bf16[256,2560]{1,0:T(8,128)(2,1)S(1)}, bf16[256,2560]{1,0:T(8,128)(2,1)}, u32[]{:S(2)}) %copy-start.2) | copy-done | bytes 1310744
  4.9 0.0 copy-start.3
  4.9 1.0 copy-done.3
  5.9 0.0 copy-start.4
  5.9 0.7 copy-done.4
  6.6 0.0 copy-start.5
  6.6 0.7 copy-done.5
  7.3 0.0 copy-start.6
  7.3 0.7 copy-done.6
  8.0 0.0 copy-start.7
  8.0 0.7 copy-done.7
  8.7 0.0 copy-start.8
  8.7 0.7 copy-done.8
  9.4 0.0 copy-start.9
  9.4 0.7 copy-done.9
  10.1 0.0 copy-start.10
  10.1 0.7 copy-done.10
  10.7 95.0 %shard_map.118 = bf16[32,160]{1,0:T(8,128)(2,1)S(1)} custom-call(bf16[32,160]{1,0:T(8,128)(2,1)S(1)} %bitcast.3, f32[1,2560]{1,0:T(1,128)S(1)} %reshape.10.gain_hbm, bf16[2560,256]{1,0:T(8,128)(2,1)S(1)} %copy-done.1, bf16[64,2560]{1,0:T(8,128)(2,1)S(1)} %copy-done.3, bf16[256,2560]{1,0:T(8,128)(2,1)S(1)} %copy-done.2, bf16[2,2560]{1,0:T(2,128)(2,1)S(1)} %copy-done.5, ...), custom_call_target="tpu_custom_call" | custom-call | tf_op jit(solution)/shard_map/pallas_call | solution.py:349
  105.8 0.6 copy.14
Async XLA Ops:
  0.7 1.6 %copy-start = (bf16[8,128,1024]{2,1,0:T(8,128)(2,1)S(1)}, bf16[8,128,1024]{2,1,0:T(8,128)(2,1)}, u32[]{:S(2)}) copy-start(bf16[8,128,1024]{2,1,0:T(8,128)(2,1)} %kv_hbm.1) | copy-start | bytes 6291460
  2.3 1.3 %copy-start.1 = (bf16[2560,256]{1,0:T(8,128)(2,1)S(1)}, bf16[2560,256]{1,0:T(8,128)(2,1)}, u32[]{:S(2)}) copy-start(bf16[2560,256]{1,0:T(8,128)(2,1)} %wq_hbm.1) | copy-start | bytes 3932164
  3.6 1.3 %copy-start.2 = (bf16[256,2560]{1,0:T(8,128)(2,1)S(1)}, bf16[256,2560]{1,0:T(8,128)(2,1)}, u32[]{:S(2)}) copy-start(bf16[256,2560]{1,0:T(8,128)(2,1)} %wo_hbm.1) | copy-start | bytes 3932164
  4.9 1.0 copy-start.3
  5.9 0.7 copy-start.4
  6.6 0.7 copy-start.5
  7.3 0.7 copy-start.6
  8.0 0.7 copy-start.7
  8.7 0.7 copy-start.8
  9.4 0.7 copy-start.9
  10.1 0.7 copy-start.10

commit v2 on v1

v2 whole, which is shorter than its diff:
```python
import jax
import jax.numpy as jnp
from jax import lax
from jax.experimental import pallas as pl
from jax.experimental.pallas import tpu as pltpu
from jax.sharding import PartitionSpec as P

HQ = 32
KVH = 4
HD = 128
STEPS = 4
SEQ = 8
D = 2560
NT = 16
NR = 32
RANK = 64
FEAT = D // NT
TOK = STEPS * SEQ
POS = 128
ROWS = TOK * 2
GROUP = HQ // KVH
CHUNKS = D // 128

adapter_scale = 2.0
norm_eps = 1e-06
masked_score = -1e30

F32 = jnp.float32
BF16 = jnp.bfloat16
MESH = pl.DeviceIdType.MESH


def dot(a, b):
    return jnp.dot(a, b, preferred_element_type=F32)


def dot_nt(a, b):
    return lax.dot_general(a, b, (((1,), (1,)), ((), ())), preferred_element_type=F32)


def split(x):
    hi = x.astype(BF16)
    return hi, (x - hi.astype(F32)).astype(BF16)


def iota(shape, dim):
    return lax.broadcasted_iota(jnp.int32, shape, dim)


def kernel(
    hid_hbm, gain_hbm, wq_hbm, wkv_hbm, wo_hbm, qif_hbm, bq_hbm, ao_hbm, bo_hbm, own_hbm, len_hbm, kv_hbm,
    out_ref,
    hid, gain, wq, wkv, wo, wide, narrow, own, lens, kv,
    hid_all, asm, pack, ad_send, ad_all, ad_f32, qi_mat, bq_mat, ao_mat, bo_mat,
    qf32, q_send, q_all, fresh_send, fresh_all,
    o_send, o_all, st_mat, st_send, st_all, mix, e_send, e_mid, e_comb, e_near, e_far,
    ld, b_s, b_r, a_s, a_r, x_s, x_r, k_s, k_r, q_s, q_r, f_s, f_r, o_s, o_r, t_s, t_r, e_s, m_r, n_s, n_r, far_r,
):
    t = lax.axis_index("tensor")
    r = lax.axis_index("replica")
    z = t // 4
    y = lax.rem(t, 4)
    zs = [z] + [lax.rem(z + d, 4) for d in range(1, 4)]
    ys = [y] + [lax.rem(y + d, 4) for d in range(1, 4)]

    pairs = [
        (hid_hbm, hid), (qif_hbm, wide.at[0]), (bq_hbm, narrow.at[0]), (ao_hbm, narrow.at[1]), (bo_hbm, wide.at[1]),
        (own_hbm, own), (len_hbm, lens), (gain_hbm, gain), (wq_hbm, wq), (wkv_hbm, wkv), (wo_hbm, wo),
    ]
    load = [pltpu.make_async_copy(a, b, ld.at[i]) for i, (a, b) in enumerate(pairs)]
    for c in load:
        c.start()

    barrier = pltpu.get_barrier_semaphore()
    near = lax.rem(r, 8)
    replica_peers = [r - near + lax.rem(near + d, 8) for d in range(1, 8)]
    replica_peers += [lax.rem(r + 8 * d, NR) for d in range(1, 4)]
    for d in range(1, NT):
        pl.semaphore_signal(barrier, inc=1, device_id={"tensor": lax.rem(t + d, NT)}, device_id_type=MESH)
    for peer in replica_peers:
        pl.semaphore_signal(barrier, inc=1, device_id={"replica": peer}, device_id_type=MESH)

    for c in load[1:5]:
        c.wait()
    for j in range(2):
        pack[...] = jnp.zeros_like(pack)
        x = wide[j].astype(F32)
        for c in range(CHUNKS):
            pack[2 * c : 2 * c + 2, :] = x[:, 128 * c : 128 * c + 128]
        w = narrow[j].astype(F32)
        for c in range(2):
            pack[2 * (CHUNKS + c) : 2 * (CHUNKS + c) + 2, :] = w[:, 128 * c : 128 * c + 128]
        ad_send[j] = pack[...].astype(BF16)
    load[0].wait()
    pl.semaphore_wait(barrier, NT - 1 + len(replica_peers))

    sends = []

    def remote(src, dst, ss, rs, peer, axis="tensor"):
        c = pltpu.make_async_remote_copy(
            src_ref=src, dst_ref=dst, send_sem=ss, recv_sem=rs, device_id={axis: peer}, device_id_type=MESH
        )
        c.start()
        sends.append(c)

    maybe = []

    def anywhere(src, dst, ss, rs, peer):
        c = pltpu.make_async_remote_copy(
            src_ref=src, dst_ref=dst, send_sem=ss, recv_sem=rs, device_id={"tensor": peer}, device_id_type=MESH
        )

        @pl.when(peer != t)
        def _():
            c.start()

        @pl.when(peer == t)
        def _():
            pltpu.make_async_copy(src, dst, rs).start()

        maybe.append((peer, c))

    def arrived(ref, sem):
        pltpu.make_async_copy(ref, ref, sem).wait()

    for d in (2, 1, 3, 0):
        remote(hid, hid_all.at[t], b_s.at[d], b_r.at[t], zs[2] * 4 + ys[d])
    for d in (1, 3):
        remote(hid, hid_all.at[t], b_s.at[3 + d], b_r.at[t], zs[d] * 4 + y)
    for d in (2, 1, 3):
        remote(hid, hid_all.at[t], b_s.at[6 + d], b_r.at[t], z * 4 + ys[d])
    pltpu.make_async_copy(hid, hid_all.at[t], b_r.at[t]).start()

    def adapters_near(j):
        for d in range(1, 8):
            peer = r - near + lax.rem(near + d, 8)
            remote(ad_send.at[j], ad_all.at[j, r], a_s.at[j, d], a_r.at[j, near], peer, "replica")
        pltpu.make_async_copy(ad_send.at[j], ad_all.at[j, r], a_r.at[j, near]).start()

    def adapters_across(j):
        base = r - near
        for s in range(8):
            arrived(ad_all.at[j, base + s], a_r.at[j, s])
        mine = ad_all.at[j, pl.ds(base, 8)]
        for d in (2, 1, 3):
            remote(mine, mine, x_s.at[j, d], x_r.at[j, r // 8], lax.rem(r + 8 * d, NR), "replica")

    def take_adapters(j, wide_mat, narrow_mat):
        for d in range(1, 4):
            group = lax.rem(r // 8 + d, 4)
            arrived(ad_all.at[j, pl.ds(group * 8, 8)], x_r.at[j, group])
        for s in range(NR):
            ad_f32[48 * s : 48 * s + 48, :] = ad_all[j, s].astype(F32)
        for c in range(CHUNKS + 2):
            rows = [ad_f32[pl.ds(2 * c + i, NR, stride=48), :] for i in range(2)]
            block = jnp.concatenate(rows, axis=0).astype(BF16)
            if c < CHUNKS:
                wide_mat[:, 128 * c : 128 * c + 128] = block
            else:
                narrow_mat[:, 128 * (c - CHUNKS) : 128 * (c - CHUNKS) + 128] = block

    adapters_near(0)

    for d in (2, 1, 3, 0):
        for j in range(2):
            src = kv_hbm.at[:, :, pl.ds(pl.multiple_of((j * KVH + ys[d]) * HD, HD), HD)]
            dst = kv.at[j, :, y]
            if d == 0:
                pltpu.make_async_copy(src, dst, k_r.at[j, y]).start()
            else:
                remote(src, dst, k_s.at[j, d], k_r.at[j, y], z * 4 + ys[d])

    for d in (1, 3):
        block = zs[d] * 4 + y
        arrived(hid_all.at[block], b_r.at[block])
        for e in (2, 1, 3):
            remote(hid_all.at[block], hid_all.at[block], b_s.at[8 + 2 * d + e], b_r.at[block], z * 4 + ys[e])

    adapters_across(0)
    adapters_near(1)

    for c in load[5:]:
        c.wait()

    label = iota((RANK, RANK), 0)
    label = lax.rem(label, NR) * 2 + label // NR
    first = (label == own[0:1, :]).astype(F32).astype(BF16)
    second = (label == own[1:2, :]).astype(F32).astype(BF16)
    paired = (dot_nt(first, second) * adapter_scale).astype(BF16)

    for e in range(4):
        for d in range(4):
            if e == 0 and d in (1, 3):
                continue
            block = zs[d] * 4 + ys[e]
            arrived(hid_all.at[block], b_r.at[block])
    squares = jnp.zeros((TOK, 1), F32)
    for s in range(NT):
        x = hid_all[s].astype(F32)
        asm[:, FEAT * s : FEAT * (s + 1)] = x
        squares = squares + jnp.sum(x * x, axis=1, keepdims=True)
    spread = lax.rsqrt(squares * (1.0 / D) + norm_eps)
    normed = jnp.concatenate(
        [
            (asm[:, 128 * c : 128 * c + 128] * spread * gain[c : c + 1, :]).astype(BF16)
            for c in range(CHUNKS)
        ],
        axis=1,
    )

    queries = dot(normed, wq[...])
    fresh = dot_nt(normed, wkv[...]).astype(BF16).astype(F32)
    take_adapters(0, qi_mat, bq_mat)
    low_hi, low_lo = split(dot_nt(normed, qi_mat[...]))
    lifted = dot(paired, bq_mat[...]).astype(BF16)
    queries = queries + (dot(low_hi, lifted) + dot(low_lo, lifted))

    for n in range(STEPS):
        for h in range(2):
            qf32[pl.ds(n * 2 + h, SEQ, stride=8), :] = queries[n * SEQ : (n + 1) * SEQ, h * HD : (h + 1) * HD]
    q_send[...] = qf32[...].astype(BF16)
    for d in (2, 1, 3, 0):
        anywhere(q_send, q_all.at[y], q_s.at[d], q_r.at[y], zs[d] * 4 + z)

    zeros = jnp.zeros((TOK, 64), F32)
    left = jnp.concatenate([fresh, zeros], axis=1)
    right = jnp.concatenate([zeros, fresh], axis=1)
    half = lax.rem(t, 2)
    fresh_send[...] = jnp.where(half == 0, left, right).astype(BF16)
    slot = (t // 8) * 2 + half
    head_row = lax.rem(t, 8) // 2
    for e in range(4):
        anywhere(fresh_send, fresh_all.at[slot], f_s.at[e], f_r.at[slot], head_row * 4 + e)

    adapters_across(1)

    score_scale = HD ** (-0.5)
    position = iota((GROUP * STEPS, 4 * POS), 1) + z * (4 * POS)
    usables = [position < lens[s] for s in range(SEQ)]
    for j in range(2):
        for e in range(4):
            arrived(kv.at[j, :, ys[e]], k_r.at[j, ys[e]])
    for e in range(4):
        arrived(q_all.at[e], q_r.at[e])
    rows = [q_all[e].astype(F32) for e in range(4)]
    scores = []
    for s in range(SEQ):
        lhs = jnp.concatenate([rows[e][8 * s : 8 * s + 8, :] for e in range(4)], axis=0).astype(BF16)
        keys = kv[0, s].reshape(4 * POS, HD)
        scores.append(jnp.where(usables[s], dot_nt(lhs, keys) * score_scale, masked_score))
    tops = [jnp.max(x, axis=1, keepdims=True) for x in scores]
    weights = [jnp.where(usables[s], jnp.exp(scores[s] - tops[s]), 0.0) for s in range(SEQ)]
    totals = [jnp.sum(x, axis=1, keepdims=True) for x in weights]
    values = [dot(weights[s].astype(BF16), kv[1, s].reshape(4 * POS, HD)) for s in range(SEQ)]
    lane = iota((2 * ROWS, 128), 1)
    stats = jnp.zeros((2 * ROWS, 128), F32)
    for e in range(4):
        part = slice(8 * e, 8 * e + 8)
        o_send[e] = jnp.concatenate([v[part, :] for v in values], axis=0).astype(BF16)
        column = jnp.concatenate([v[part, :] for v in tops] + [v[part, :] for v in totals], axis=0)
        stats = jnp.where(lane == e, column, stats)
    stats = jnp.transpose(stats)
    for e in range(4):
        st_send[e] = stats[e : e + 1, :]
    for e in range(4):
        anywhere(o_send.at[e], o_all.at[z], o_s.at[e], o_r.at[z], y * 4 + e)
        anywhere(st_send.at[e], st_all.at[z], t_s.at[e], t_r.at[z], y * 4 + e)

    for j in range(4):
        arrived(fresh_all.at[j], f_r.at[j])
    new_keys = fresh_all[0] + fresh_all[1]
    new_values = fresh_all[2] + fresh_all[3]
    row = iota((ROWS, TOK), 0)
    col = iota((ROWS, TOK), 1)
    causal = (lax.rem(col, SEQ) == row // 8) & (col // SEQ <= lax.rem(row, 8) // 2)
    recent = jnp.where(causal, dot_nt(q_send[...], new_keys) * score_scale, masked_score)
    recent_top = jnp.max(recent, axis=1, keepdims=True)

    take_adapters(1, bo_mat, ao_mat)
    lifted_out = dot(paired, bo_mat[...]).astype(BF16)
    wide_mat = qi_mat
    wide_mat[...] = lifted_out

    for d in range(4):
        arrived(st_all.at[d], t_r.at[d])
    st_mat[...] = jnp.full_like(st_mat, masked_score)
    for d in range(4):
        st_mat[d : d + 1, :] = st_all[d]
    stats = jnp.transpose(st_mat[...])
    valid = iota((ROWS, 128), 1) < 4
    tops = stats[0:ROWS, :]
    totals = jnp.where(valid, stats[ROWS : 2 * ROWS, :], 0.0)
    peak = jnp.maximum(jnp.max(tops, axis=1, keepdims=True), recent_top)
    factor = jnp.where(valid, jnp.exp(tops - peak), 0.0)
    recent_weights = jnp.where(causal, jnp.exp(recent - peak), 0.0)
    total = jnp.sum(totals * factor, axis=1, keepdims=True) + jnp.sum(recent_weights, axis=1, keepdims=True)
    acc = dot(recent_weights.astype(BF16), new_values)
    for d in range(4):
        arrived(o_all.at[d], o_r.at[d])
        acc = acc + o_all[d].astype(F32) * factor[:, d : d + 1]
    mix[...] = acc / total
    mixed = jnp.concatenate(
        [
            jnp.concatenate([mix[pl.ds(n * 2 + h, SEQ, stride=8), :] for h in range(2)], axis=1)
            for n in range(STEPS)
        ],
        axis=0,
    ).astype(BF16)

    low_hi, low_lo = split(dot_nt(mixed, ao_mat[...]))

    def project(d):
        cols = pl.ds(pl.multiple_of(zs[d] * (4 * FEAT), 128), 4 * FEAT)
        lifted = wide_mat[:, cols]
        block = dot(mixed, wo[:, cols]) + (dot(low_hi, lifted) + dot(low_lo, lifted))
        for e in range(4):
            e_send[4 * d + e] = block[:, FEAT * e : FEAT * (e + 1)].astype(BF16)

    project(2)
    for e in range(4):
        remote(e_send.at[8 + e], e_far.at[y], e_s.at[8 + e], far_r.at[y], zs[2] * 4 + e)
    for d in (1, 3, 0):
        project(d)
        for e in (2, 1, 3):
            remote(e_send.at[4 * d + ys[e]], e_mid.at[d, y], e_s.at[4 * d + e], m_r.at[d, y], z * 4 + ys[e])

    def along_y(d):
        total = e_send[4 * d + y].astype(F32)
        for e in (1, 3, 2):
            arrived(e_mid.at[d, ys[e]], m_r.at[d, ys[e]])
            total = total + e_mid[d, ys[e]].astype(F32)
        return total

    for d in (1, 3):
        e_comb[d] = along_y(d).astype(BF16)
        remote(e_comb.at[d], e_near.at[d], n_s.at[d], n_r.at[d], zs[d] * 4 + y)
    summed = along_y(0)
    for d in (1, 3):
        arrived(e_near.at[d], n_r.at[d])
        summed = summed + e_near[d].astype(F32)
    for e in range(4):
        arrived(e_far.at[e], far_r.at[e])
        summed = summed + e_far[e].astype(F32)
    out_ref[...] = summed.astype(BF16)

    for c in sends:
        c.wait_send()
    for peer, c in maybe:

        @pl.when(peer != t)
        def _():
            c.wait_send()


def body(
    hidden_in, norm_gain, w_query, w_keyval, w_out, query_input_factor, b_query, a_out, b_out,
    component_owner_rows, lengths, kv_cache,
):
    dma = pltpu.SemaphoreType.DMA
    vmem = pltpu.VMEM
    scratch = [
        vmem((TOK, FEAT), BF16),
        vmem((CHUNKS, 128), F32),
        vmem((D, 256), BF16),
        vmem((64, D), BF16),
        vmem((256, D), BF16),
        vmem((2, 2, D), BF16),
        vmem((2, 2, 256), BF16),
        vmem((2, RANK), jnp.int32),
        pltpu.SMEM((SEQ,), jnp.int32),
        vmem((2, SEQ, 4, POS, HD), BF16),
        vmem((NT, TOK, FEAT), BF16),
        vmem((TOK, D), F32),
        vmem((48, 128), F32),
        vmem((2, 48, 128), BF16),
        vmem((2, NR, 48, 128), BF16),
        vmem((NR * 48, 128), F32),
        vmem((RANK, D), BF16),
        vmem((RANK, 256), BF16),
        vmem((RANK, 256), BF16),
        vmem((RANK, D), BF16),
        vmem((ROWS, HD), F32),
        vmem((ROWS, HD), BF16),
        vmem((4, ROWS, HD), BF16),
        vmem((TOK, 128), BF16),
        vmem((4, TOK, 128), BF16),
        vmem((4, ROWS, HD), BF16),
        vmem((4, ROWS, HD), BF16),
        vmem((128, 128), F32),
        vmem((4, 1, 128), F32),
        vmem((4, 1, 128), F32),
        vmem((ROWS, HD), F32),
        vmem((NT, TOK, FEAT), BF16),
        vmem((4, 4, TOK, FEAT), BF16),
        vmem((4, TOK, FEAT), BF16),
        vmem((4, TOK, FEAT), BF16),
        vmem((4, TOK, FEAT), BF16),
        dma((11,)),
        dma((18,)), dma((NT,)),
        dma((2, 8)), dma((2, 8)),
        dma((2, 4)), dma((2, 4)),
        dma((2, 4)), dma((2, 4)),
        dma((4,)), dma((4,)),
        dma((4,)), dma((4,)),
        dma((4,)), dma((4,)),
        dma((4,)), dma((4,)),
        dma((NT,)), dma((4, 4)),
        dma((4,)), dma((4,)),
        dma((4,)),
    ]
    out = pl.pallas_call(
        kernel,
        out_shape=jax.ShapeDtypeStruct((TOK, FEAT), BF16),
        in_specs=[pl.BlockSpec(memory_space=pl.ANY)] * 12,
        out_specs=pl.BlockSpec(memory_space=pltpu.VMEM),
        scratch_shapes=scratch,
        compiler_params=pltpu.CompilerParams(collective_id=0, has_side_effects=True, vmem_limit_bytes=62 << 20),
    )(
        hidden_in.reshape(TOK, FEAT), norm_gain.reshape(CHUNKS, 128), w_query, w_keyval, w_out, query_input_factor, b_query,
        a_out, b_out, component_owner_rows, lengths, kv_cache,
    )
    return out.reshape(STEPS, SEQ, FEAT)


def solution(mesh):
    return jax.shard_map(
        body,
        mesh=mesh,
        in_specs=(
            P(None, "replica", "tensor"),
            P(),
            P(None, "tensor"),
            P("tensor", None),
            P("tensor", None),
            P("replica", None),
            P("replica", "tensor"),
            P("replica", "tensor"),
            P("replica", None),
            P(),
            P("replica"),
            P("replica", "tensor", None),
        ),
        out_specs=P(None, "replica", "tensor"),
        check_vma=False,
    )
```

time: 107 us -> 77.6 us (0.73)
  the two profiles are of different devices: /device:TPU:32 before, /device:TPU:2 now
where the time goes in v2:
time: 77.6 us; the launch traced here: 77.4 us
  Pallas kernels  76 us (98%)
  local copies, waits for them, and re-layouts  1.32 us (2%)
    pallas_call x1, Pallas kernels, body(): pl.pallas_call(kernel, out_shape=jax.ShapeDtypeStruct((TOK, FEAT), BF16),...  76 us

profile of v2, /device:TPU:2, one launch (start us, length us, event | category | flops | bytes accessed | tf_op | source)
XLA Modules:
  0.0 77.4 jit_solution(4237377838531031597)
XLA Ops:
  0.0 76.0 %shard_map.118 = bf16[32,160]{1,0:T(8,128)(2,1)} custom-call(bf16[32,160]{1,0:T(8,128)(2,1)} %bitcast.4, f32[20,128]{1,0:T(8,128)} %bitcast.5, bf16[2560,256]{1,0:T(8,128)(2,1)} %wq_hbm.1, bf16[64,2560]{1,0:T(8,128)(2,1)} %wkv_hbm.1, bf16[256,2560]{1,0:T(8,128)(2,1)} %wo_hbm.1, bf16[2,2560]{1,0:T(2,128)(2,1)} %qif_hbm.1, bf16[2,256]{1,0:T(2,128)(2,1)} %bq_hbm.1, ...), custom_call_target="tpu_custom_call" | custom-call | tf_op jit(solution)/shard_map/pallas_call | solution.py:411
  76.0 1.3 %copy.14 = bf16[4,8,160]{2,1,0:T(8,128)(2,1)} copy(bf16[4,8,160]{2,1,0:T(8,128)(2,1)} %bitcast.3) | data formatting | bytes 20480

commit v3 on v2

--- a/solution.py
+++ b/solution.py
@@ -52,9 +52,8 @@
     out_ref,
     hid, gain, wq, wkv, wo, wide, narrow, own, lens, kv,
     hid_all, asm, pack, ad_send, ad_all, ad_f32, qi_mat, bq_mat, ao_mat, bo_mat,
-    qf32, q_send, q_all, fresh_send, fresh_all,
-    o_send, o_all, st_mat, st_send, st_all, mix, e_send, e_mid, e_comb, e_near, e_far,
-    ld, b_s, b_r, a_s, a_r, x_s, x_r, k_s, k_r, q_s, q_r, f_s, f_r, o_s, o_r, t_s, t_r, e_s, m_r, n_s, n_r, far_r,
+    qf32, q_send, q_all, o_send, o_mid, o_comb, o_near, st_mat, mix, e_send, e_mid, e_comb, e_near, e_far,
+    ld, b_s, b_r, a_s, a_r, x_s, x_r, q_s, q_r, o_s, om_r, on_s, on_r, e_s, m_r, n_s, n_r, far_r,
 ):
     t = lax.axis_index("tensor")
     r = lax.axis_index("replica")
@@ -65,7 +64,7 @@
 
     pairs = [
         (hid_hbm, hid), (qif_hbm, wide.at[0]), (bq_hbm, narrow.at[0]), (ao_hbm, narrow.at[1]), (bo_hbm, wide.at[1]),
-        (own_hbm, own), (len_hbm, lens), (gain_hbm, gain), (wq_hbm, wq), (wkv_hbm, wkv), (wo_hbm, wo),
+        (own_hbm, own), (len_hbm, lens), (gain_hbm, gain), (wq_hbm, wq), (wkv_hbm, wkv), (kv_hbm, kv), (wo_hbm, wo),
     ]
     load = [pltpu.make_async_copy(a, b, ld.at[i]) for i, (a, b) in enumerate(pairs)]
     for c in load:
@@ -75,8 +74,9 @@
     near = lax.rem(r, 8)
     replica_peers = [r - near + lax.rem(near + d, 8) for d in range(1, 8)]
     replica_peers += [lax.rem(r + 8 * d, NR) for d in range(1, 4)]
-    for d in range(1, NT):
-        pl.semaphore_signal(barrier, inc=1, device_id={"tensor": lax.rem(t + d, NT)}, device_id_type=MESH)
+    tensor_peers = [zs[d] * 4 + ys[e] for d in (1, 3) for e in range(4)] + [z * 4 + ys[e] for e in range(1, 4)]
+    for peer in tensor_peers:
+        pl.semaphore_signal(barrier, inc=1, device_id={"tensor": peer}, device_id_type=MESH)
     for peer in replica_peers:
         pl.semaphore_signal(barrier, inc=1, device_id={"replica": peer}, device_id_type=MESH)
 
@@ -92,7 +92,7 @@
             pack[2 * (CHUNKS + c) : 2 * (CHUNKS + c) + 2, :] = w[:, 128 * c : 128 * c + 128]
         ad_send[j] = pack[...].astype(BF16)
     load[0].wait()
-    pl.semaphore_wait(barrier, NT - 1 + len(replica_peers))
+    pl.semaphore_wait(barrier, len(tensor_peers) + len(replica_peers))
 
     sends = []
 
@@ -103,32 +103,13 @@
         c.start()
         sends.append(c)
 
-    maybe = []
-
-    def anywhere(src, dst, ss, rs, peer):
-        c = pltpu.make_async_remote_copy(
-            src_ref=src, dst_ref=dst, send_sem=ss, recv_sem=rs, device_id={"tensor": peer}, device_id_type=MESH
-        )
-
-        @pl.when(peer != t)
-        def _():
-            c.start()
-
-        @pl.when(peer == t)
-        def _():
-            pltpu.make_async_copy(src, dst, rs).start()
-
-        maybe.append((peer, c))
-
     def arrived(ref, sem):
         pltpu.make_async_copy(ref, ref, sem).wait()
 
-    for d in (2, 1, 3, 0):
-        remote(hid, hid_all.at[t], b_s.at[d], b_r.at[t], zs[2] * 4 + ys[d])
     for d in (1, 3):
-        remote(hid, hid_all.at[t], b_s.at[3 + d], b_r.at[t], zs[d] * 4 + y)
+        remote(hid, hid_all.at[t], b_s.at[d], b_r.at[t], zs[d] * 4 + y)
     for d in (2, 1, 3):
-        remote(hid, hid_all.at[t], b_s.at[6 + d], b_r.at[t], z * 4 + ys[d])
+        remote(hid, hid_all.at[t], b_s.at[3 + d], b_r.at[t], z * 4 + ys[d])
     pltpu.make_async_copy(hid, hid_all.at[t], b_r.at[t]).start()
 
     def adapters_near(j):
@@ -161,20 +142,14 @@
 
     adapters_near(0)
 
-    for d in (2, 1, 3, 0):
-        for j in range(2):
-            src = kv_hbm.at[:, :, pl.ds(pl.multiple_of((j * KVH + ys[d]) * HD, HD), HD)]
-            dst = kv.at[j, :, y]
-            if d == 0:
-                pltpu.make_async_copy(src, dst, k_r.at[j, y]).start()
-            else:
-                remote(src, dst, k_s.at[j, d], k_r.at[j, y], z * 4 + ys[d])
-
     for d in (1, 3):
         block = zs[d] * 4 + y
-        arrived(hid_all.at[block], b_r.at[block])
+        held = hid_all.at[block]
+        arrived(held, b_r.at[block])
+        for e in (0, 1) if d == 1 else (2, 3):
+            remote(held, held, b_s.at[4 + 4 * d + e], b_r.at[block], zs[4 - d] * 4 + ys[e])
         for e in (2, 1, 3):
-            remote(hid_all.at[block], hid_all.at[block], b_s.at[8 + 2 * d + e], b_r.at[block], z * 4 + ys[e])
+            remote(held, held, b_s.at[19 + 3 * (d // 2) + e], b_r.at[block], z * 4 + ys[e])
 
     adapters_across(0)
     adapters_near(1)
@@ -182,6 +157,7 @@
     for c in load[5:]:
         c.wait()
 
+    st_mat[...] = jnp.zeros_like(st_mat)
     label = iota((RANK, RANK), 0)
     label = lax.rem(label, NR) * 2 + label // NR
     first = (label == own[0:1, :]).astype(F32).astype(BF16)
@@ -218,62 +194,114 @@
     for n in range(STEPS):
         for h in range(2):
             qf32[pl.ds(n * 2 + h, SEQ, stride=8), :] = queries[n * SEQ : (n + 1) * SEQ, h * HD : (h + 1) * HD]
-    q_send[...] = qf32[...].astype(BF16)
-    for d in (2, 1, 3, 0):
-        anywhere(q_send, q_all.at[y], q_s.at[d], q_r.at[y], zs[d] * 4 + z)
-
-    zeros = jnp.zeros((TOK, 64), F32)
-    left = jnp.concatenate([fresh, zeros], axis=1)
-    right = jnp.concatenate([zeros, fresh], axis=1)
-    half = lax.rem(t, 2)
-    fresh_send[...] = jnp.where(half == 0, left, right).astype(BF16)
-    slot = (t // 8) * 2 + half
-    head_row = lax.rem(t, 8) // 2
-    for e in range(4):
-        anywhere(fresh_send, fresh_all.at[slot], f_s.at[e], f_r.at[slot], head_row * 4 + e)
+    q_send[0:ROWS, :] = qf32[...].astype(BF16)
+    q_send[ROWS : ROWS + 16, :] = jnp.concatenate([fresh[0:16, :], fresh[16:32, :]], axis=1).astype(BF16)
+    for d in (2, 1, 3):
+        remote(q_send, q_all.at[t], q_s.at[d], q_r.at[t], zs[d] * 4 + y)
+    for e in (2, 1, 3):
+        remote(q_send, q_all.at[t], q_s.at[3 + e], q_r.at[t], z * 4 + ys[e])
+    pltpu.make_async_copy(q_send, q_all.at[t], q_r.at[t]).start()
+
+    def hand_on(d):
+        block = zs[d] * 4 + y
+        held = q_all.at[block]
+        arrived(held, q_r.at[block])
+        for e in (2, 1, 3):
+            remote(held, held, q_s.at[4 + 3 * d + e - 1], q_r.at[block], z * 4 + ys[e])
 
     adapters_across(1)
 
     score_scale = HD ** (-0.5)
-    position = iota((GROUP * STEPS, 4 * POS), 1) + z * (4 * POS)
+    position = iota((GROUP * STEPS, POS), 1) + t * POS
     usables = [position < lens[s] for s in range(SEQ)]
-    for j in range(2):
+    lane = iota((2 * ROWS, 128), 1)
+
+    def put(ref, out, row):
+        high = row.astype(BF16)
+        rest = row - high.astype(F32)
+        middle = rest.astype(BF16)
+        low = (rest - middle.astype(F32)).astype(BF16)
+        ref[0:ROWS, :] = out.astype(BF16)
+        pieces = [high.astype(F32), middle.astype(F32), low.astype(F32), jnp.zeros((13, 128), F32)]
+        ref[ROWS : ROWS + 16, :] = jnp.concatenate(pieces, axis=0).astype(BF16)
+
+    def get(ref):
+        pieces = ref[ROWS : ROWS + 16, :].astype(F32)
+        return ref[0:ROWS, :].astype(F32), pieces[0:1, :] + pieces[1:2, :] + pieces[2:3, :]
+
+    def attend(d):
+        k = zs[d]
+        rows = [q_all[4 * k + e, 0:ROWS, :].astype(F32) for e in range(4)]
+        key_lanes = pl.ds(pl.multiple_of(k * HD, HD), HD)
+        value_lanes = pl.ds(pl.multiple_of((KVH + k) * HD, HD), HD)
+        scores = []
+        for s in range(SEQ):
+            lhs = jnp.concatenate([rows[e][8 * s : 8 * s + 8, :] for e in range(4)], axis=0).astype(BF16)
+            scores.append(jnp.where(usables[s], dot_nt(lhs, kv[s, :, key_lanes]) * score_scale, masked_score))
+        tops = [jnp.max(x, axis=1, keepdims=True) for x in scores]
+        weights = [jnp.where(usables[s], jnp.exp(scores[s] - tops[s]), 0.0) for s in range(SEQ)]
+        totals = [jnp.sum(x, axis=1, keepdims=True) for x in weights]
+        values = [dot(weights[s].astype(BF16), kv[s, :, value_lanes]) for s in range(SEQ)]
+        stats = jnp.zeros((2 * ROWS, 128), F32)
         for e in range(4):
-            arrived(kv.at[j, :, ys[e]], k_r.at[j, ys[e]])
-    for e in range(4):
-        arrived(q_all.at[e], q_r.at[e])
-    rows = [q_all[e].astype(F32) for e in range(4)]
-    scores = []
-    for s in range(SEQ):
-        lhs = jnp.concatenate([rows[e][8 * s : 8 * s + 8, :] for e in range(4)], axis=0).astype(BF16)
-        keys = kv[0, s].reshape(4 * POS, HD)
-        scores.append(jnp.where(usables[s], dot_nt(lhs, keys) * score_scale, masked_score))
-    tops = [jnp.max(x, axis=1, keepdims=True) for x in scores]
-    weights = [jnp.where(usables[s], jnp.exp(scores[s] - tops[s]), 0.0) for s in range(SEQ)]
-    totals = [jnp.sum(x, axis=1, keepdims=True) for x in weights]
-    values = [dot(weights[s].astype(BF16), kv[1, s].reshape(4 * POS, HD)) for s in range(SEQ)]
-    lane = iota((2 * ROWS, 128), 1)
-    stats = jnp.zeros((2 * ROWS, 128), F32)
-    for e in range(4):
-        part = slice(8 * e, 8 * e + 8)
-        o_send[e] = jnp.concatenate([v[part, :] for v in values], axis=0).astype(BF16)
-        column = jnp.concatenate([v[part, :] for v in tops] + [v[part, :] for v in totals], axis=0)
-        stats = jnp.where(lane == e, column, stats)
-    stats = jnp.transpose(stats)
-    for e in range(4):
-        st_send[e] = stats[e : e + 1, :]
-    for e in range(4):
-        anywhere(o_send.at[e], o_all.at[z], o_s.at[e], o_r.at[z], y * 4 + e)
-        anywhere(st_send.at[e], st_all.at[z], t_s.at[e], t_r.at[z], y * 4 + e)
-
-    for j in range(4):
-        arrived(fresh_all.at[j], f_r.at[j])
-    new_keys = fresh_all[0] + fresh_all[1]
-    new_values = fresh_all[2] + fresh_all[3]
+            part = slice(8 * e, 8 * e + 8)
+            column = jnp.concatenate([v[part, :] for v in tops] + [v[part, :] for v in totals], axis=0)
+            stats = jnp.where(lane == e, column, stats)
+        stats = jnp.transpose(stats)
+        for e in range(4):
+            part = slice(8 * e, 8 * e + 8)
+            put(o_send.at[d, e], jnp.concatenate([v[part, :] for v in values], axis=0), stats[e : e + 1, :])
+        for e in (2, 1, 3):
+            remote(o_send.at[d, ys[e]], o_mid.at[d, y], o_s.at[d, e], om_r.at[d, y], z * 4 + ys[e])
+
+    def take_queries(d):
+        for e in range(0 if d == 0 else 1, 4):
+            block = zs[d] * 4 + ys[e]
+            arrived(q_all.at[block], q_r.at[block])
+
+    take_queries(0)
+    attend(0)
+    hand_on(1)
+    hand_on(3)
+    hand_on(2)
+    take_queries(1)
+    attend(1)
+    take_queries(3)
+    attend(3)
+    take_queries(2)
+    attend(2)
+
+    def along_y_values(d):
+        for e in range(1, 4):
+            arrived(o_mid.at[d, ys[e]], om_r.at[d, ys[e]])
+        return [get(o_send.at[d, y])] + [get(o_mid.at[d, ys[e]]) for e in range(1, 4)]
+
+    row_lane = iota((1, 128), 1)
+    for d in (1, 3, 2):
+        parts = along_y_values(d)
+        rows = [row for _, row in parts]
+        top = jnp.maximum(jnp.maximum(rows[0], rows[1]), jnp.maximum(rows[2], rows[3]))
+        factors = [jnp.exp(row - top) for row in rows]
+        total = sum(f * pltpu.roll(row, ROWS, 1) for f, row in zip(factors, rows))
+        st_mat[0:4, :] = jnp.concatenate(factors, axis=0)
+        columns = jnp.transpose(st_mat[...])
+        acc = sum(parts[i][0] * columns[0:ROWS, i : i + 1] for i in range(4))
+        put(o_comb.at[d], acc, jnp.where(row_lane < ROWS, top, pltpu.roll(total, ROWS, 1)))
+        remote(o_comb.at[d], o_near.at[d], on_s.at[d], on_r.at[d], zs[d] * 4 + y)
+
+    def halves(first):
+        a = q_all[first, ROWS : ROWS + 16, :].astype(F32)
+        b = q_all[first + 1, ROWS : ROWS + 16, :].astype(F32)
+        upper = jnp.concatenate([a[:, 0:64], b[:, 0:64]], axis=1)
+        lower = jnp.concatenate([a[:, 64:128], b[:, 64:128]], axis=1)
+        return jnp.concatenate([upper, lower], axis=0).astype(BF16)
+
+    new_keys = halves(2 * z)
+    new_values = halves(8 + 2 * z)
     row = iota((ROWS, TOK), 0)
     col = iota((ROWS, TOK), 1)
     causal = (lax.rem(col, SEQ) == row // 8) & (col // SEQ <= lax.rem(row, 8) // 2)
-    recent = jnp.where(causal, dot_nt(q_send[...], new_keys) * score_scale, masked_score)
+    recent = jnp.where(causal, dot_nt(q_send[0:ROWS, :], new_keys) * score_scale, masked_score)
     recent_top = jnp.max(recent, axis=1, keepdims=True)
 
     take_adapters(1, bo_mat, ao_mat)
@@ -281,23 +309,23 @@
     wide_mat = qi_mat
     wide_mat[...] = lifted_out
 
-    for d in range(4):
-        arrived(st_all.at[d], t_r.at[d])
-    st_mat[...] = jnp.full_like(st_mat, masked_score)
-    for d in range(4):
-        st_mat[d : d + 1, :] = st_all[d]
+    parts = along_y_values(0)
+    for d in (1, 3, 2):
+        arrived(o_near.at[d], on_r.at[d])
+        parts.append(get(o_near.at[d]))
+    count = len(parts)
+    st_mat[0:count, :] = jnp.concatenate([row for _, row in parts], axis=0)
     stats = jnp.transpose(st_mat[...])
-    valid = iota((ROWS, 128), 1) < 4
-    tops = stats[0:ROWS, :]
+    valid = iota((ROWS, 128), 1) < count
+    tops = jnp.where(valid, stats[0:ROWS, :], masked_score)
     totals = jnp.where(valid, stats[ROWS : 2 * ROWS, :], 0.0)
     peak = jnp.maximum(jnp.max(tops, axis=1, keepdims=True), recent_top)
     factor = jnp.where(valid, jnp.exp(tops - peak), 0.0)
     recent_weights = jnp.where(causal, jnp.exp(recent - peak), 0.0)
     total = jnp.sum(totals * factor, axis=1, keepdims=True) + jnp.sum(recent_weights, axis=1, keepdims=True)
     acc = dot(recent_weights.astype(BF16), new_values)
-    for d in range(4):
-        arrived(o_all.at[d], o_r.at[d])
-        acc = acc + o_all[d].astype(F32) * factor[:, d : d + 1]
+    for i in range(count):
+        acc = acc + parts[i][0] * factor[:, i : i + 1]
     mix[...] = acc / total
     mixed = jnp.concatenate(
         [
@@ -345,11 +373,6 @@
 
     for c in sends:
         c.wait_send()
-    for peer, c in maybe:
-
-        @pl.when(peer != t)
-        def _():
-            c.wait_send()
 
 
 def body(
@@ -368,7 +391,7 @@
         vmem((2, 2, 256), BF16),
         vmem((2, RANK), jnp.int32),
         pltpu.SMEM((SEQ,), jnp.int32),
-        vmem((2, SEQ, 4, POS, HD), BF16),
+        vmem((SEQ, POS, 1024), BF16),
         vmem((NT, TOK, FEAT), BF16),
         vmem((TOK, D), F32),
         vmem((48, 128), F32),
@@ -380,29 +403,25 @@
         vmem((RANK, 256), BF16),
         vmem((RANK, D), BF16),
         vmem((ROWS, HD), F32),
-        vmem((ROWS, HD), BF16),
-        vmem((4, ROWS, HD), BF16),
-        vmem((TOK, 128), BF16),
-        vmem((4, TOK, 128), BF16),
-        vmem((4, ROWS, HD), BF16),
-        vmem((4, ROWS, HD), BF16),
+        vmem((ROWS + 16, HD), BF16),
+        vmem((NT, ROWS + 16, HD), BF16),
+        vmem((4, 4, ROWS + 16, HD), BF16),
+        vmem((4, 4, ROWS + 16, HD), BF16),
+        vmem((4, ROWS + 16, HD), BF16),
+        vmem((4, ROWS + 16, HD), BF16),
         vmem((128, 128), F32),
-        vmem((4, 1, 128), F32),
-        vmem((4, 1, 128), F32),
         vmem((ROWS, HD), F32),
         vmem((NT, TOK, FEAT), BF16),
         vmem((4, 4, TOK, FEAT), BF16),
         vmem((4, TOK, FEAT), BF16),
         vmem((4, TOK, FEAT), BF16),
         vmem((4, TOK, FEAT), BF16),
-        dma((11,)),
-        dma((18,)), dma((NT,)),
+        dma((12,)),
+        dma((27,)), dma((NT,)),
         dma((2, 8)), dma((2, 8)),
         dma((2, 4)), dma((2, 4)),
-        dma((2, 4)), dma((2, 4)),
-        dma((4,)), dma((4,)),
-        dma((4,)), dma((4,)),
-        dma((4,)), dma((4,)),
+        dma((NT,)), dma((NT,)),
+        dma((4, 4)), dma((4, 4)),
         dma((4,)), dma((4,)),
         dma((NT,)), dma((4, 4)),
         dma((4,)), dma((4,)),

time: 77.6 us -> 66.2 us (0.85)
  the two profiles are of different devices: /device:TPU:2 before, /device:TPU:32 now
where the time goes in v3:
time: 66.2 us; the launch traced here: 65.9 us
  Pallas kernels  64.6 us (98%)
  local copies, waits for them, and re-layouts  1.32 us (2%)
    pallas_call x1, Pallas kernels, body(): pl.pallas_call(kernel, out_shape=jax.ShapeDtypeStruct((TOK, FEAT), BF16),...  64.6 us
    unnamed x1, local copies, waits for them, and re-layouts  1.32 us

profile of v3, /device:TPU:32, one launch (start us, length us, event | category | flops | bytes accessed | tf_op | source)
XLA Modules:
  0.0 65.9 jit_solution(3954378970819394514)
XLA Ops:
  0.0 64.6 %shard_map.118 = bf16[32,160]{1,0:T(8,128)(2,1)} custom-call(bf16[32,160]{1,0:T(8,128)(2,1)} %bitcast.4, f32[20,128]{1,0:T(8,128)} %bitcast.5, bf16[2560,256]{1,0:T(8,128)(2,1)} %wq_hbm.1, bf16[64,2560]{1,0:T(8,128)(2,1)} %wkv_hbm.1, bf16[256,2560]{1,0:T(8,128)(2,1)} %wo_hbm.1, bf16[2,2560]{1,0:T(2,128)(2,1)} %qif_hbm.1, bf16[2,256]{1,0:T(2,128)(2,1)} %bq_hbm.1, ...), custom_call_target="tpu_custom_call" | custom-call | tf_op jit(solution)/shard_map/pallas_call | solution.py:430
  64.6 1.3 %copy.14 = bf16[4,8,160]{2,1,0:T(8,128)(2,1)} copy(bf16[4,8,160]{2,1,0:T(8,128)(2,1)} %bitcast.3) | data formatting | bytes 20480
